TPU v7x, 128 devices: a whole 4x4x4 slice. The times are simulated.
128 devices in a mesh: fsdp: 64 (over z_lo, y, x, core), rep: 2 (over z_hi).
Axes of the slice: x: 4, y: 4, z: 4 (z_hi: 2, z_lo: 2; z = z_hi * 2 + z_lo), core: 2. Of those that a mesh axis runs over, the one named last changes fastest.
Arguments:
- gate_up: bfloat16 [8, 7168, 4096], P(None, ('fsdp', 'rep')), may hold values from -2 to 2
- expert_owner: int32 [8], replicated, may hold values from 0 to 7, each once
Outputs:
- rollout_weights: bfloat16 [64, 7168, 512], P('fsdp')
- block_scale: float32 [64, 56, 4], P('fsdp')
Inputs may be any that keep to these rules, and one draw needn't show every extreme that they name: `expert_owner`: each of the 8 rollout groups owns exactly one expert.
All inputs are finite; a program needn't handle non-finite values. Where the computation divides by a largest or mean magnitude, that divisor is 1e-20 or more.
Results may differ from a plain program's by a relative error of at most 0.001.
Values may be sent and summed in bfloat16 or wider, within the bound.
No kernel may reach another device: no remote copies, remote signals or barrier semaphores. Data moves between devices by JAX's collectives and lax.ppermute only.
A program may use at most 128 MiB of HBM per device.

v0:
```python
import jax
import jax.numpy as jnp
from jax import lax
from jax.sharding import PartitionSpec as P

GRP = 8
BLOCK = 128


epsilon = 1e-06


def on_device(gate_up, expert_owner):
    experts, rows_dev, width = gate_up.shape
    replicas = lax.axis_size("rep")
    shard = width // 2 // GRP
    columns = 2 * shard
    expert_ids = jnp.arange(experts, dtype=jnp.int32)
    owned = jnp.sum(
        expert_ids[:, None] * (expert_owner[:, None] == expert_ids[None, :]).astype(jnp.int32),
        axis=0,
    )
    ordered = jnp.take(gate_up, owned, axis=0)
    outgoing = (
        ordered.reshape(experts, rows_dev, 2, GRP, shard)
        .transpose(0, 3, 1, 2, 4)
        .reshape(experts * GRP, rows_dev, columns)
    )
    received = lax.all_to_all(outgoing, "fsdp", split_axis=0, concat_axis=0, tiled=True)
    sources = received.shape[0]
    total_rows = sources * rows_dev * replicas
    bands = total_rows // BLOCK
    col_blocks = columns // BLOCK
    whole_raw = lax.all_gather(
        received.reshape(sources, 1, rows_dev, columns), "rep", axis=1, tiled=True
    )
    blocks = whole_raw.reshape(bands, BLOCK, col_blocks, BLOCK)
    peaks = jnp.max(jnp.abs(blocks), axis=(1, 3)).astype(jnp.float32)
    whole = (
        (blocks.astype(jnp.float32) / (peaks[:, None, :, None] + epsilon))
        .astype(jnp.bfloat16)
        .reshape(total_rows, columns)
    )
    return (whole[None], peaks[None])


def solution(mesh):
    placed = (P(None, ("fsdp", "rep"), None), P())
    return jax.shard_map(
        on_device,
        mesh=mesh,
        in_specs=placed,
        out_specs=(P("fsdp", None, None), P("fsdp", None, None)),
        check_vma=False,
    )
```

profile of v0, /device:TPU:1, one launch (start us, length us, event | category | flops | bytes accessed | tf_op | source)
XLA Modules:
  0.0 248.4 jit_solution(597682684647562479)
XLA Ops:
  7.2 0.0 all-gather.3.cloned.1.call-start
  7.2 0.7 select_reduce_fusion
  8.0 4.7 %gather_fusion = bf16[8,56,4096]{2,1,0:T(8,128)(2,1)} fusion(bf16[8,56,4096]{2,1,0:T(8,128)(2,1)} %param.2, s32[1024]{0:T(1024)S(1)} %pad_clamp_fusion), kind=kCustom, calls=%fused_computation | custom fusion | bytes 7340064 | tf_op jit(solution)/shard_map/jit(_take)/gather | solution.py:23
  12.6 3.3 %copy.10 = bf16[56,8,16,256]{3,2,1,0:T(8,128)(2,1)S(1)} copy(bf16[56,8,16,256]{3,1,2,0:T(8,128)(2,1)} %bitcast.18) | data formatting | bytes 7340032
  15.9 0.4 select_bitcast_fusion
  16.3 4.7 %copy.8 = bf16[8,8,56,2,256]{4,3,2,1,0:T(2,128)(2,1)} copy(bf16[8,8,56,2,256]{4,1,3,2,0:T(8,128)(2,1)S(1)} %select_bitcast_fusion) | data formatting | bytes 7340032 | tf_op jit(solution)/shard_map/transpose | solution.py:26
  21.0 7.0 %reshape.74 = bf16[64,56,512]{2,1,0:T(8,128)(2,1)} reshape(bf16[8,8,56,2,256]{4,3,2,1,0:T(2,128)(2,1)} %copy.8) | data formatting | bytes 7340032 | tf_op jit(solution)/shard_map/reshape | solution.py:27
  28.0 55.9 %all_to_all.5 = bf16[64,56,512]{2,1,0:T(8,128)(2,1)} all-to-all(bf16[64,56,512]{2,1,0:T(8,128)(2,1)} %reshape.74), channel_id=1, replica_groups=mesh['fsdp'=64,'rep'=2] {'fsdp'}, dimensions={0} | all-to-all | bytes 7340032 | tf_op jit(solution)/shard_map/all_to_all | solution.py:29
  83.9 0.0 all-gather.3.cloned.1.call-update
  83.9 95.8 %all-gather.3.cloned.1.call-done = bf16[64,112,512]{2,1,0:T(8,128)(2,1)} async-done(((bf16[64,56,512]{2,1,0:T(8,128)(2,1)}), bf16[64,112,512]{2,1,0:T(8,128)(2,1)}) %all-gather.3.cloned.1.call-update) | async-done | bytes 7340048 | tf_op jit(solution)/shard_map/all_gather | solution.py:34
  179.7 8.0 %abs.8 = bf16[64,112,512]{2,1,0:T(8,128)(2,1)} abs(bf16[64,112,512]{2,1,0:T(8,128)(2,1)} %all-gather.3.cloned.1.call-done) | non-fusion elementwise | flops 3670016 | bytes 14680064 | tf_op jit(solution)/shard_map/abs | solution.py:38
  187.7 11.1 %abs.7 = bf16[56,128,4,128]{3,2,1,0:T(4,128)(2,1)} reshape(bf16[64,112,512]{2,1,0:T(8,128)(2,1)} %abs.8) | data formatting | bytes 14680064 | tf_op jit(solution)/shard_map/abs | solution.py:38
  198.9 6.1 %reduce_max.9 = bf16[56,4]{1,0:T(8,128)(2,1)S(1)} reduce(bf16[56,128,4,128]{3,2,1,0:T(4,128)(2,1)} %abs.7, bf16[]{:T(256)} %constant.20.clone.1), dimensions={1,3}, to_apply=%region_1.2 | reduce | flops 3669792 | bytes 7340482 | tf_op jit(solution)/shard_map/reduce_max | solution.py:38
  204.9 0.7 copy.9
  205.6 7.1 %div.17 = f32[56,128,4,128]{3,2,1,0:T(4,128)} broadcast(f32[56,4]{1,0:T(8,128)S(1)} %convert_add_fusion), dimensions={0,2} | broadcast | bytes 14680960 | tf_op jit(solution)/shard_map/div | solution.py:40
  212.7 17.5 %div.18 = f32[1,7168,512]{2,1,0:T(8,128)} reshape(f32[56,128,4,128]{3,2,1,0:T(4,128)} %div.17) | data formatting | bytes 29360128 | tf_op jit(solution)/shard_map/div | solution.py:40
  230.2 11.4 %fusion = bf16[1,7168,512]{2,1,0:T(8,128)(2,1)} fusion(f32[1,7168,512]{2,1,0:T(8,128)} %div.18, bf16[1,7168,512]{2,1,0:T(8,128)(2,1)} %bitcast.16), kind=kLoop, calls=%fused_computation.2 | loop fusion | flops 11010048 | bytes 29360128 | tf_op jit(solution)/shard_map/convert_element_type | solution.py:41
  (5 shorter events, 0.0 us)
Async XLA Ops:
  7.2 172.5 %all-gather.3.cloned.1.call-start = ((), (), s32[]{:S(2)}) async-start(), calls=%async_computation.1 | async-start | bytes 11010048 | tf_op jit(solution)/shard_map/all_gather | solution.py:34
Sparse Core Ops, SparseCore 0:
  84.0 95.6 all-gather.2
where the time goes:
time: 250 us; the launch traced here: 248 us
  waiting for transfers between devices  95.8 us (38%)
  local copies, waits for them, and re-layouts  56 us (22%)
  blocking collectives  55.9 us (22%)
  other arithmetic  26.6 us (11%)
  between operations  14.1 us (6%)
    all_gather x1, waiting for transfers between devices, on_device(): lax.all_gather(received.reshape(sources, 1, rows_dev, columns), 'rep', ax...  95.8 us
    all_to_all x1, blocking collectives, on_device(): lax.all_to_all(outgoing, 'fsdp', split_axis=0, concat_axis=0, tiled=True)  55.9 us
    div x2, local copies, waits for them, and re-layouts, on_device(): blocks.astype(jnp.float32) / (peaks[:, None, :, None] + epsilon)  24.6 us
    convert_element_type x1, other arithmetic, on_device(): whole = (blocks.astype(jnp.float32) / (peaks[:, None, :, None] + epsilon)...  11.4 us
    abs x1, local copies, waits for them, and re-layouts, on_device(): peaks = jnp.max(jnp.abs(blocks), axis=(1, 3)).astype(jnp.float32)  11.1 us
    abs x1, other arithmetic, on_device(): peaks = jnp.max(jnp.abs(blocks), axis=(1, 3)).astype(jnp.float32)  8.02 us
    reshape x1, local copies, waits for them, and re-layouts, on_device(): outgoing = ordered.reshape(experts, rows_dev, 2, GRP, shard).transpose(0,...  6.97 us
    reduce_max x1, other arithmetic, on_device(): peaks = jnp.max(jnp.abs(blocks), axis=(1, 3)).astype(jnp.float32)  6.06 us
  transfers between devices with their start and end apart: 1, of which 1 were waited for; matrix products, arithmetic and copies ran while one was open for 0% of the time, Pallas kernels for 0%

commit v1 on v0

v1 whole, which is shorter than its diff:
```python
import jax
import jax.numpy as jnp
from jax import lax
from jax.experimental import pallas as pl
from jax.experimental.pallas import tpu as pltpu
from jax.sharding import PartitionSpec as P

GRP = 8
BLOCK = 128
BANDS = 8

epsilon = 1e-06


def arrange_kernel(owned_ref, x_ref, o_ref):
    del owned_ref
    shard = x_ref.shape[2] // 2 // GRP
    copies = o_ref.shape[0] // GRP
    for j in range(GRP):
        for half in range(2):
            part = x_ref[0, :, pl.ds((half * GRP + j) * shard, shard)]
            for r in range(copies):
                o_ref[j * copies + r, :, pl.ds(half * shard, shard)] = part


def arrange(owned, gate_up, copies):
    experts, rows, width = gate_up.shape
    columns = width // GRP
    return pl.pallas_call(
        arrange_kernel,
        out_shape=jax.ShapeDtypeStruct((experts * GRP * copies, rows, columns), gate_up.dtype),
        grid_spec=pltpu.PrefetchScalarGridSpec(
            num_scalar_prefetch=1,
            grid=(experts,),
            in_specs=[pl.BlockSpec((1, rows, width), lambda g, owned: (owned[g], 0, 0))],
            out_specs=pl.BlockSpec((GRP * copies, rows, columns), lambda g, owned: (g, 0, 0)),
        ),
        compiler_params=pltpu.CompilerParams(vmem_limit_bytes=32 * 2**20),
        name="arrange",
    )(owned, gate_up)


def scale_kernel(x_ref, o_ref, s_ref):
    columns = x_ref.shape[1]
    for b in range(BANDS):
        rows = pl.ds(b * BLOCK, BLOCK)
        peaks = []
        for c in range(columns // BLOCK):
            lanes = pl.ds(c * BLOCK, BLOCK)
            x = x_ref[rows, lanes]
            top = jnp.max(jnp.abs(x).astype(jnp.float32), axis=0, keepdims=True)
            peak = jnp.max(top, axis=1, keepdims=True)
            inverse = 1.0 / (peak + epsilon)
            o_ref[rows, lanes] = (x.astype(jnp.float32) * inverse).astype(o_ref.dtype)
            peaks.append(peak)
        s_ref[b : b + 1, :] = jnp.concatenate(peaks, axis=1)


def scale_blocks(x):
    rows, columns = x.shape
    step = BANDS * BLOCK
    return pl.pallas_call(
        scale_kernel,
        out_shape=(
            jax.ShapeDtypeStruct((rows, columns), x.dtype),
            jax.ShapeDtypeStruct((rows // BLOCK, columns // BLOCK), jnp.float32),
        ),
        grid=(rows // step,),
        in_specs=[pl.BlockSpec((step, columns), lambda i: (i, 0))],
        out_specs=(
            pl.BlockSpec((step, columns), lambda i: (i, 0)),
            pl.BlockSpec((BANDS, columns // BLOCK), lambda i: (i, 0)),
        ),
        compiler_params=pltpu.CompilerParams(vmem_limit_bytes=32 * 2**20),
        name="scale_blocks",
    )(x)


def on_device(gate_up, expert_owner):
    experts, rows_dev, width = gate_up.shape
    columns = width // GRP
    devices = lax.axis_size(("fsdp", "rep"))
    expert_ids = jnp.arange(experts, dtype=jnp.int32)
    owned = jnp.sum(
        expert_ids[:, None] * (expert_owner[:, None] == expert_ids[None, :]).astype(jnp.int32),
        axis=0,
    )
    outgoing = arrange(owned, gate_up, lax.axis_size("rep"))
    received = lax.all_to_all(outgoing, ("fsdp", "rep"), split_axis=0, concat_axis=0, tiled=True)
    whole, peaks = scale_blocks(received.reshape(devices * rows_dev, columns))
    return (whole[None], peaks[None])


def solution(mesh):
    placed = (P(None, ("fsdp", "rep"), None), P())
    return jax.shard_map(
        on_device,
        mesh=mesh,
        in_specs=placed,
        out_specs=(P("fsdp", None, None), P("fsdp", None, None)),
        check_vma=False,
    )
```

time: 250 us -> 108 us (0.43)
  waiting for transfers between devices: 95.8 us -> 0 us
  local copies, waits for them, and re-layouts: 56 us -> 2.69 us
  blocking collectives: 55.9 us -> 97 us
  other arithmetic: 26.6 us -> 0.74 us
  between operations: 14.1 us -> 0.64 us
  Pallas kernels: 0 us -> 6.94 us
    all_gather x1 -> x0, waiting for transfers between devices: 95.8 us -> none  [on_device(): lax.all_gather(received.reshape(sources, 1, rows_dev, columns), 'rep', ax...]
    all_to_all x1, blocking collectives: 55.9 us -> 97 us  [on_device(): lax.all_to_all(outgoing, ('fsdp', 'rep'), split_axis=0, concat_axis=0, ti...]
    div x2 -> x0, local copies, waits for them, and re-layouts: 24.6 us -> none  [on_device(): blocks.astype(jnp.float32) / (peaks[:, None, :, None] + epsilon)]
    convert_element_type x2 -> x0, other arithmetic: 11.4 us -> none  [the longest x1 11.4 us: on_device(): whole = (blocks.astype(jnp.float32) / (peaks[:, None, :, None] + epsilon)...]
    abs x1 -> x0, local copies, waits for them, and re-layouts: 11.1 us -> none  [on_device(): peaks = jnp.max(jnp.abs(blocks), axis=(1, 3)).astype(jnp.float32)]
    abs x1 -> x0, other arithmetic: 8.02 us -> none  [on_device(): peaks = jnp.max(jnp.abs(blocks), axis=(1, 3)).astype(jnp.float32)]
    reshape x1 -> x0, local copies, waits for them, and re-layouts: 6.97 us -> none  [on_device(): outgoing = ordered.reshape(experts, rows_dev, 2, GRP, shard).transpose(0,...]
    pallas_call x0 -> x2, Pallas kernels: none -> 6.94 us  [the longest x1 5.79 us: scale_blocks(): pl.pallas_call(scale_kernel, out_shape=(jax.ShapeDtypeStruct((rows, colum...]
  transfers between devices with their start and end apart: 1 -> 0, of which waited for: 1 -> 0; matrix products, arithmetic and copies ran while one was open for 0% -> 0% of each run, Pallas kernels for 0% -> 0%
where the time goes in v1:
time: 108 us
  blocking collectives  97 us (90%)
  Pallas kernels  6.94 us (6%)
  local copies, waits for them, and re-layouts  2.69 us (2%)
    all_to_all x1, blocking collectives, on_device(): lax.all_to_all(outgoing, ('fsdp', 'rep'), split_axis=0, concat_axis=0, ti...  97 us
    pallas_call x1, Pallas kernels, scale_blocks(): pl.pallas_call(scale_kernel, out_shape=(jax.ShapeDtypeStruct((rows, colum...  5.79 us
    unnamed x3, local copies, waits for them, and re-layouts  2.69 us

profile of v1, /device:TPU:1, one launch (start us, length us, event | category | flops | bytes accessed | tf_op | source)
XLA Modules:
  0.0 108.0 jit_solution(11380595686787817238)
XLA Ops:
  0.6 0.7 select_reduce_fusion.owned_ref
  1.4 0.0 copy-start
  1.4 2.0 %copy-done = bf16[8,56,4096]{2,1,0:T(8,128)(2,1)S(1)} copy-done((bf16[8,56,4096]{2,1,0:T(8,128)(2,1)S(1)}, bf16[8,56,4096]{2,1,0:T(8,128)(2,1)}, u32[]{:S(2)}) %copy-start) | copy-done | bytes 3670040
  3.4 1.2 %arrange.1 = bf16[128,56,512]{2,1,0:T(8,128)(2,1)S(1)} custom-call(s32[8]{0:T(128)S(1)} %select_reduce_fusion.owned_ref, bf16[8,56,4096]{2,1,0:T(8,128)(2,1)S(1)} %copy-done), custom_call_target="tpu_custom_call" | custom-call | tf_op jit(solution)/shard_map/arrange/pallas_call | solution.py:29
  4.6 97.0 %all_to_all.5 = bf16[128,56,512]{2,1,0:T(8,128)(2,1)S(1)} all-to-all(bf16[128,56,512]{2,1,0:T(8,128)(2,1)S(1)} %arrange.1), channel_id=1, replica_groups=mesh['fsdp'=64,'rep'=2] {'fsdp','rep'}, dimensions={0} | all-to-all | bytes 14680064 | tf_op jit(solution)/shard_map/all_to_all | solution.py:89
  101.5 5.8 %scale_blocks.1 = (bf16[7168,512]{1,0:T(8,128)(2,1)}, f32[56,4]{1,0:T(8,128)S(1)}) custom-call(bf16[7168,512]{1,0:T(8,128)(2,1)S(1)} %bitcast.3), custom_call_target="tpu_custom_call" | custom-call | tf_op jit(solution)/shard_map/scale_blocks/pallas_call | solution.py:62
  107.3 0.7 copy.5
Async XLA Ops:
  1.4 2.0 %copy-start = (bf16[8,56,4096]{2,1,0:T(8,128)(2,1)S(1)}, bf16[8,56,4096]{2,1,0:T(8,128)(2,1)}, u32[]{:S(2)}) copy-start(bf16[8,56,4096]{2,1,0:T(8,128)(2,1)} %x_ref.1) | copy-start | bytes 11010052

commit v2 on v1

v2 whole, which is shorter than its diff:
```python
import jax
import jax.numpy as jnp
from jax import lax
from jax.experimental import pallas as pl
from jax.experimental.pallas import tpu as pltpu
from jax.sharding import PartitionSpec as P

GRP = 8
BLOCK = 128
BANDS = 8

epsilon = 1e-06


def arrange_kernel(owner_ref, x_ref, o_ref):
    experts = x_ref.shape[0]
    shard = x_ref.shape[2] // 2 // GRP
    copies = o_ref.shape[0] // GRP // experts

    def regroup(g, carry):
        expert = jnp.int32(0)
        for e in range(experts):
            expert = expert + jnp.where(owner_ref[e] == g, e, 0)
        for j in range(GRP):
            for half in range(2):
                part = x_ref[expert, :, pl.ds((half * GRP + j) * shard, shard)]
                for r in range(copies):
                    o_ref[(g * GRP + j) * copies + r, :, pl.ds(half * shard, shard)] = part
        return carry

    lax.fori_loop(0, experts, regroup, 0)


def arrange(expert_owner, gate_up, copies):
    experts, rows, width = gate_up.shape
    columns = width // GRP
    return pl.pallas_call(
        arrange_kernel,
        out_shape=jax.ShapeDtypeStruct((experts * GRP * copies, rows, columns), gate_up.dtype),
        in_specs=[
            pl.BlockSpec(memory_space=pltpu.SMEM),
            pl.BlockSpec(memory_space=pltpu.VMEM),
        ],
        out_specs=pl.BlockSpec(memory_space=pltpu.VMEM),
        compiler_params=pltpu.CompilerParams(vmem_limit_bytes=32 * 2**20),
        name="arrange",
    )(expert_owner, gate_up)


def scale_kernel(x_ref, o_ref, s_ref, scaled, peaks_ref, sems):
    rows, columns = x_ref.shape
    step = BANDS * BLOCK
    steps = rows // step

    def copy_out(i):
        part = pl.ds(pl.multiple_of(i * step, step), step)
        return pltpu.make_async_copy(scaled.at[part], o_ref.at[part], sems.at[i])

    def scale_step(i, carry):
        start = pl.multiple_of(i * step, step)
        tops = []
        for b in range(BANDS):
            top = jnp.abs(x_ref[pl.ds(start + b * BLOCK, 16), :])
            for r in range(16, BLOCK, 16):
                top = jnp.maximum(top, jnp.abs(x_ref[pl.ds(start + b * BLOCK + r, 16), :]))
            tops.append(jnp.max(top.astype(jnp.float32), axis=0, keepdims=True))
        tops = jnp.concatenate(tops, axis=0)

        peaks = []
        for c in range(columns // BLOCK):
            lanes = pl.ds(c * BLOCK, BLOCK)
            peak = jnp.max(tops[:, c * BLOCK : (c + 1) * BLOCK], axis=1, keepdims=True)
            inverse = 1.0 / (peak + epsilon)
            for b in range(BANDS):
                band = pl.ds(start + b * BLOCK, BLOCK)
                scaled[band, lanes] = (x_ref[band, lanes].astype(jnp.float32) * inverse[b : b + 1]).astype(scaled.dtype)
            peaks.append(peak)
        copy_out(i).start()
        peaks_ref[pl.ds(pl.multiple_of(i * BANDS, BANDS), BANDS), : columns // BLOCK] = jnp.concatenate(peaks, axis=1)
        return carry

    lax.fori_loop(0, steps, scale_step, 0)
    s_ref[...] = peaks_ref[...].T[: s_ref.shape[0], : s_ref.shape[1]]
    for i in range(steps):
        copy_out(i).wait()


def scale_blocks(x):
    rows, columns = x.shape
    return pl.pallas_call(
        scale_kernel,
        out_shape=(
            jax.ShapeDtypeStruct((rows, columns), x.dtype),
            jax.ShapeDtypeStruct((columns // BLOCK, rows // BLOCK), jnp.float32),
        ),
        in_specs=[pl.BlockSpec(memory_space=pltpu.VMEM)],
        out_specs=(
            pl.BlockSpec(memory_space=pl.ANY),
            pl.BlockSpec(memory_space=pltpu.VMEM),
        ),
        scratch_shapes=[
            pltpu.VMEM((rows, columns), x.dtype),
            pltpu.VMEM((BLOCK, BLOCK), jnp.float32),
            pltpu.SemaphoreType.DMA((rows // (BANDS * BLOCK),)),
        ],
        compiler_params=pltpu.CompilerParams(vmem_limit_bytes=32 * 2**20),
        name="scale_blocks",
    )(x)


def on_device(gate_up, expert_owner):
    rows_dev, width = gate_up.shape[1:]
    devices = lax.axis_size(("fsdp", "rep"))
    outgoing = arrange(expert_owner, gate_up, lax.axis_size("rep"))
    received = lax.all_to_all(outgoing, ("fsdp", "rep"), split_axis=0, concat_axis=0, tiled=True)
    whole, peaks = scale_blocks(received.reshape(devices * rows_dev, width // GRP))
    return (whole[None], peaks.T[None])


def solution(mesh):
    placed = (P(None, ("fsdp", "rep"), None), P())
    return jax.shard_map(
        on_device,
        mesh=mesh,
        in_specs=placed,
        out_specs=(P("fsdp", None, None), P("fsdp", None, None)),
        check_vma=False,
    )
```

time: 108 us -> 106 us (0.981)
  Pallas kernels: 6.94 us -> 5.69 us
    pallas_call x1, Pallas kernels: 5.79 us -> 4.57 us  [scale_blocks(): pl.pallas_call(scale_kernel, out_shape=(jax.ShapeDtypeStruct((rows, colum...]
    unnamed x3 -> x4, local copies, waits for them, and re-layouts: 2.69 us -> 2.69 us
where the time goes in v2:
time: 106 us
  blocking collectives  97 us (92%)
  Pallas kernels  5.69 us (5%)
  local copies, waits for them, and re-layouts  2.69 us (3%)
    all_to_all x1, blocking collectives, on_device(): lax.all_to_all(outgoing, ('fsdp', 'rep'), split_axis=0, concat_axis=0, ti...  97 us
    pallas_call x1, Pallas kernels, scale_blocks(): pl.pallas_call(scale_kernel, out_shape=(jax.ShapeDtypeStruct((rows, colum...  4.57 us
    unnamed x4, local copies, waits for them, and re-layouts  2.69 us

profile of v2, /device:TPU:1, one launch (start us, length us, event | category | flops | bytes accessed | tf_op | source)
XLA Modules:
  0.0 106.0 jit_solution(3042799896200790156)
XLA Ops:
  0.6 0.0 copy-start
  0.6 2.0 %copy-done = bf16[8,56,4096]{2,1,0:T(8,128)(2,1)S(1)} copy-done((bf16[8,56,4096]{2,1,0:T(8,128)(2,1)S(1)}, bf16[8,56,4096]{2,1,0:T(8,128)(2,1)}, u32[]{:S(2)}) %copy-start) | copy-done | bytes 3670040
  2.7 0.0 copy-start.1
  2.7 0.7 copy-done.1
  3.3 1.1 %arrange.1 = bf16[128,56,512]{2,1,0:T(8,128)(2,1)S(1)} custom-call(s32[8]{0:T(128)S(1)} %copy-done.1, bf16[8,56,4096]{2,1,0:T(8,128)(2,1)S(1)} %copy-done), custom_call_target="tpu_custom_call" | custom-call | tf_op jit(solution)/shard_map/arrange/pallas_call | solution.py:37
  4.5 97.0 %all_to_all.5 = bf16[128,56,512]{2,1,0:T(8,128)(2,1)S(1)} all-to-all(bf16[128,56,512]{2,1,0:T(8,128)(2,1)S(1)} %arrange.1), channel_id=1, replica_groups=mesh['fsdp'=64,'rep'=2] {'fsdp','rep'}, dimensions={0} | all-to-all | bytes 14680064 | tf_op jit(solution)/shard_map/all_to_all | solution.py:115
  101.4 4.6 %scale_blocks.1 = (bf16[7168,512]{1,0:T(8,128)(2,1)}, f32[4,56]{1,0:T(4,128)}) custom-call(bf16[7168,512]{1,0:T(8,128)(2,1)S(1)} %bitcast.5), custom_call_target="tpu_custom_call" | custom-call | tf_op jit(solution)/shard_map/scale_blocks/pallas_call | solution.py:90
Async XLA Ops:
  0.6 2.0 %copy-start = (bf16[8,56,4096]{2,1,0:T(8,128)(2,1)S(1)}, bf16[8,56,4096]{2,1,0:T(8,128)(2,1)}, u32[]{:S(2)}) copy-start(bf16[8,56,4096]{2,1,0:T(8,128)(2,1)} %x_ref.1) | copy-start | bytes 11010052
  2.7 0.7 copy-start.1

commit v3 on v2

--- a/solution.py
+++ b/solution.py
@@ -12,18 +12,25 @@
 epsilon = 1e-06
 
 
-def arrange_kernel(owner_ref, x_ref, o_ref):
+def arrange_kernel(owner_ref, x_ref, o_ref, buf, sems):
     experts = x_ref.shape[0]
     shard = x_ref.shape[2] // 2 // GRP
     copies = o_ref.shape[0] // GRP // experts
 
-    def regroup(g, carry):
+    def fetch(g):
         expert = jnp.int32(0)
         for e in range(experts):
             expert = expert + jnp.where(owner_ref[e] == g, e, 0)
+        return pltpu.make_async_copy(x_ref.at[expert], buf.at[g], sems.at[g])
+
+    for g in range(experts):
+        fetch(g).start()
+
+    def regroup(g, carry):
+        pltpu.make_async_copy(x_ref.at[0], buf.at[g], sems.at[g]).wait()
         for j in range(GRP):
             for half in range(2):
-                part = x_ref[expert, :, pl.ds((half * GRP + j) * shard, shard)]
+                part = buf[g, :, pl.ds((half * GRP + j) * shard, shard)]
                 for r in range(copies):
                     o_ref[(g * GRP + j) * copies + r, :, pl.ds(half * shard, shard)] = part
         return carry
@@ -39,12 +46,19 @@
         out_shape=jax.ShapeDtypeStruct((experts * GRP * copies, rows, columns), gate_up.dtype),
         in_specs=[
             pl.BlockSpec(memory_space=pltpu.SMEM),
-            pl.BlockSpec(memory_space=pltpu.VMEM),
+            pl.BlockSpec(memory_space=pltpu.HBM),
         ],
         out_specs=pl.BlockSpec(memory_space=pltpu.VMEM),
+        scratch_shapes=[
+            pltpu.VMEM(gate_up.shape, gate_up.dtype),
+            pltpu.SemaphoreType.DMA((experts,)),
+        ],
         compiler_params=pltpu.CompilerParams(vmem_limit_bytes=32 * 2**20),
         name="arrange",
-    )(expert_owner, gate_up)
+    )(
+        pltpu.with_memory_space_constraint(expert_owner, pltpu.HBM),
+        pltpu.with_memory_space_constraint(gate_up, pltpu.HBM),
+    )
 
 
 def scale_kernel(x_ref, o_ref, s_ref, scaled, peaks_ref, sems):

time: 106 us -> 105 us (level)
  local copies, waits for them, and re-layouts: 2.69 us -> 0 us
  Pallas kernels: 5.69 us -> 7.37 us
    unnamed x4 -> x0, local copies, waits for them, and re-layouts: 2.69 us -> none
    pallas_call x1, Pallas kernels: 1.12 us -> 2.8 us  [arrange(): pl.pallas_call(arrange_kernel, out_shape=jax.ShapeDtypeStruct((experts *...]
where the time goes in v3:
time: 105 us
  blocking collectives  97 us (92%)
  Pallas kernels  7.37 us (7%)
    all_to_all x1, blocking collectives, on_device(): lax.all_to_all(outgoing, ('fsdp', 'rep'), split_axis=0, concat_axis=0, ti...  97 us
    pallas_call x1, Pallas kernels, scale_blocks(): pl.pallas_call(scale_kernel, out_shape=(jax.ShapeDtypeStruct((rows, colum...  4.57 us
    pallas_call x1, Pallas kernels, arrange(): pl.pallas_call(arrange_kernel, out_shape=jax.ShapeDtypeStruct((experts *...  2.8 us

profile of v3, /device:TPU:1, one launch (start us, length us, event | category | flops | bytes accessed | tf_op | source)
XLA Modules:
  0.0 105.0 jit_solution(4690166676465067594)
XLA Ops:
  0.6 2.8 %arrange.1 = bf16[128,56,512]{2,1,0:T(8,128)(2,1)S(1)} custom-call(s32[8]{0:T(128)} %owner_ref.1, bf16[8,56,4096]{2,1,0:T(8,128)(2,1)} %x_ref.1), custom_call_target="tpu_custom_call" | custom-call | tf_op jit(solution)/shard_map/arrange/pallas_call | solution.py:44
  3.4 97.0 %all_to_all.5 = bf16[128,56,512]{2,1,0:T(8,128)(2,1)S(1)} all-to-all(bf16[128,56,512]{2,1,0:T(8,128)(2,1)S(1)} %arrange.1), channel_id=1, replica_groups=mesh['fsdp'=64,'rep'=2] {'fsdp','rep'}, dimensions={0} | all-to-all | bytes 14680064 | tf_op jit(solution)/shard_map/all_to_all | solution.py:129
  100.4 4.6 %scale_blocks.1 = (bf16[7168,512]{1,0:T(8,128)(2,1)}, f32[4,56]{1,0:T(4,128)}) custom-call(bf16[7168,512]{1,0:T(8,128)(2,1)S(1)} %bitcast.5), custom_call_target="tpu_custom_call" | custom-call | tf_op jit(solution)/shard_map/scale_blocks/pallas_call | solution.py:104

commit v4 on v3

--- a/solution.py
+++ b/solution.py
@@ -12,27 +12,28 @@
 epsilon = 1e-06
 
 
-def arrange_kernel(owner_ref, x_ref, o_ref, buf, sems):
+def arrange_kernel(owner_hbm, x_ref, o_ref, owner_ref, buf, owner_sem, sems):
     experts = x_ref.shape[0]
     shard = x_ref.shape[2] // 2 // GRP
     copies = o_ref.shape[0] // GRP // experts
 
-    def fetch(g):
-        expert = jnp.int32(0)
-        for e in range(experts):
-            expert = expert + jnp.where(owner_ref[e] == g, e, 0)
-        return pltpu.make_async_copy(x_ref.at[expert], buf.at[g], sems.at[g])
+    def fetch(e):
+        return pltpu.make_async_copy(x_ref.at[e], buf.at[e], sems.at[e])
 
-    for g in range(experts):
-        fetch(g).start()
+    owners = pltpu.make_async_copy(owner_hbm, owner_ref, owner_sem)
+    owners.start()
+    for e in range(experts):
+        fetch(e).start()
+    owners.wait()
 
-    def regroup(g, carry):
-        pltpu.make_async_copy(x_ref.at[0], buf.at[g], sems.at[g]).wait()
+    def regroup(e, carry):
+        fetch(e).wait()
+        first = owner_ref[e] * (GRP * copies)
         for j in range(GRP):
             for half in range(2):
-                part = buf[g, :, pl.ds((half * GRP + j) * shard, shard)]
+                part = buf[e, :, pl.ds((half * GRP + j) * shard, shard)]
                 for r in range(copies):
-                    o_ref[(g * GRP + j) * copies + r, :, pl.ds(half * shard, shard)] = part
+                    o_ref[first + (j * copies + r), :, pl.ds(half * shard, shard)] = part
         return carry
 
     lax.fori_loop(0, experts, regroup, 0)
@@ -45,12 +46,14 @@
         arrange_kernel,
         out_shape=jax.ShapeDtypeStruct((experts * GRP * copies, rows, columns), gate_up.dtype),
         in_specs=[
-            pl.BlockSpec(memory_space=pltpu.SMEM),
+            pl.BlockSpec(memory_space=pltpu.HBM),
             pl.BlockSpec(memory_space=pltpu.HBM),
         ],
         out_specs=pl.BlockSpec(memory_space=pltpu.VMEM),
         scratch_shapes=[
+            pltpu.SMEM(expert_owner.shape, expert_owner.dtype),
             pltpu.VMEM(gate_up.shape, gate_up.dtype),
+            pltpu.SemaphoreType.DMA,
             pltpu.SemaphoreType.DMA((experts,)),
         ],
         compiler_params=pltpu.CompilerParams(vmem_limit_bytes=32 * 2**20),
@@ -70,7 +73,7 @@
         part = pl.ds(pl.multiple_of(i * step, step), step)
         return pltpu.make_async_copy(scaled.at[part], o_ref.at[part], sems.at[i])
 
-    def scale_step(i, carry):
+    def find_peaks(i):
         start = pl.multiple_of(i * step, step)
         tops = []
         for b in range(BANDS):
@@ -79,21 +82,25 @@
                 top = jnp.maximum(top, jnp.abs(x_ref[pl.ds(start + b * BLOCK + r, 16), :]))
             tops.append(jnp.max(top.astype(jnp.float32), axis=0, keepdims=True))
         tops = jnp.concatenate(tops, axis=0)
+        peaks = [
+            jnp.max(tops[:, c * BLOCK : (c + 1) * BLOCK], axis=1, keepdims=True)
+            for c in range(columns // BLOCK)
+        ]
+        peaks_ref[pl.ds(pl.multiple_of(i * BANDS, BANDS), BANDS), : columns // BLOCK] = jnp.concatenate(peaks, axis=1)
+        return tuple(1.0 / (peak + epsilon) for peak in peaks)
 
-        peaks = []
-        for c in range(columns // BLOCK):
-            lanes = pl.ds(c * BLOCK, BLOCK)
-            peak = jnp.max(tops[:, c * BLOCK : (c + 1) * BLOCK], axis=1, keepdims=True)
-            inverse = 1.0 / (peak + epsilon)
-            for b in range(BANDS):
-                band = pl.ds(start + b * BLOCK, BLOCK)
+    def scale_step(i, inverses):
+        start = pl.multiple_of(i * step, step)
+        later = find_peaks(jnp.minimum(i + 1, steps - 1))
+        for b in range(BANDS):
+            band = pl.ds(start + b * BLOCK, BLOCK)
+            for c, inverse in enumerate(inverses):
+                lanes = pl.ds(c * BLOCK, BLOCK)
                 scaled[band, lanes] = (x_ref[band, lanes].astype(jnp.float32) * inverse[b : b + 1]).astype(scaled.dtype)
-            peaks.append(peak)
         copy_out(i).start()
-        peaks_ref[pl.ds(pl.multiple_of(i * BANDS, BANDS), BANDS), : columns // BLOCK] = jnp.concatenate(peaks, axis=1)
-        return carry
+        return later
 
-    lax.fori_loop(0, steps, scale_step, 0)
+    lax.fori_loop(0, steps, scale_step, find_peaks(0))
     s_ref[...] = peaks_ref[...].T[: s_ref.shape[0], : s_ref.shape[1]]
     for i in range(steps):
         copy_out(i).wait()

time: 105 us -> 104 us (level)
  Pallas kernels: 7.37 us -> 6.2 us
where the time goes in v4:
time: 104 us
  blocking collectives  97 us (93%)
  Pallas kernels  6.2 us (6%)
    all_to_all x1, blocking collectives, on_device(): lax.all_to_all(outgoing, ('fsdp', 'rep'), split_axis=0, concat_axis=0, ti...  97 us
    pallas_call x1, Pallas kernels, scale_blocks(): pl.pallas_call(scale_kernel, out_shape=(jax.ShapeDtypeStruct((rows, colum...  4.07 us
    pallas_call x1, Pallas kernels, arrange(): pl.pallas_call(arrange_kernel, out_shape=jax.ShapeDtypeStruct((experts *...  2.13 us

profile of v4, /device:TPU:1, one launch (start us, length us, event | category | flops | bytes accessed | tf_op | source)
XLA Modules:
  0.0 103.8 jit_solution(13829014744261992789)
XLA Ops:
  0.6 2.1 %arrange.1 = bf16[128,56,512]{2,1,0:T(8,128)(2,1)S(1)} custom-call(s32[8]{0:T(128)} %owner_hbm.1, bf16[8,56,4096]{2,1,0:T(8,128)(2,1)} %x_ref.1), custom_call_target="tpu_custom_call" | custom-call | tf_op jit(solution)/shard_map/arrange/pallas_call | solution.py:45
  2.8 97.0 %all_to_all.5 = bf16[128,56,512]{2,1,0:T(8,128)(2,1)S(1)} all-to-all(bf16[128,56,512]{2,1,0:T(8,128)(2,1)S(1)} %arrange.1), channel_id=1, replica_groups=mesh['fsdp'=64,'rep'=2] {'fsdp','rep'}, dimensions={0} | all-to-all | bytes 14680064 | tf_op jit(solution)/shard_map/all_to_all | solution.py:136
  99.7 4.1 %scale_blocks.1 = (bf16[7168,512]{1,0:T(8,128)(2,1)}, f32[4,56]{1,0:T(4,128)}) custom-call(bf16[7168,512]{1,0:T(8,128)(2,1)S(1)} %bitcast.5), custom_call_target="tpu_custom_call" | custom-call | tf_op jit(solution)/shard_map/scale_blocks/pallas_call | solution.py:111

commit v5 on v4

--- a/solution.py
+++ b/solution.py
@@ -8,6 +8,7 @@
 GRP = 8
 BLOCK = 128
 BANDS = 8
+PART = 4
 
 epsilon = 1e-06
 
@@ -64,14 +65,14 @@
     )
 
 
-def scale_kernel(x_ref, o_ref, s_ref, scaled, peaks_ref, sems):
+def scale_kernel(x_ref, o_ref, s_ref, scaled, peaks_ref, table_ref, sems, table_sem):
     rows, columns = x_ref.shape
     step = BANDS * BLOCK
     steps = rows // step
 
-    def copy_out(i):
-        part = pl.ds(pl.multiple_of(i * step, step), step)
-        return pltpu.make_async_copy(scaled.at[part], o_ref.at[part], sems.at[i])
+    def copy_out(n):
+        part = pl.ds(pl.multiple_of(n * (PART * BLOCK), PART * BLOCK), PART * BLOCK)
+        return pltpu.make_async_copy(scaled.at[part], o_ref.at[part], sems.at[n])
 
     def find_peaks(i):
         start = pl.multiple_of(i * step, step)
@@ -86,7 +87,7 @@
             jnp.max(tops[:, c * BLOCK : (c + 1) * BLOCK], axis=1, keepdims=True)
             for c in range(columns // BLOCK)
         ]
-        peaks_ref[pl.ds(pl.multiple_of(i * BANDS, BANDS), BANDS), : columns // BLOCK] = jnp.concatenate(peaks, axis=1)
+        peaks_ref[i, :, : columns // BLOCK] = jnp.concatenate(peaks, axis=1)
         return tuple(1.0 / (peak + epsilon) for peak in peaks)
 
     def scale_step(i, inverses):
@@ -97,32 +98,44 @@
             for c, inverse in enumerate(inverses):
                 lanes = pl.ds(c * BLOCK, BLOCK)
                 scaled[band, lanes] = (x_ref[band, lanes].astype(jnp.float32) * inverse[b : b + 1]).astype(scaled.dtype)
-        copy_out(i).start()
+            if b % PART == PART - 1:
+                copy_out(i * (BANDS // PART) + b // PART).start()
         return later
 
     lax.fori_loop(0, steps, scale_step, find_peaks(0))
-    s_ref[...] = peaks_ref[...].T[: s_ref.shape[0], : s_ref.shape[1]]
-    for i in range(steps):
-        copy_out(i).wait()
+    table = [peaks_ref[i] for i in range(steps)] + [jnp.zeros((BLOCK - steps * BANDS, BLOCK), jnp.float32)]
+    table_ref[...] = jnp.concatenate(table, axis=0).T[: s_ref.shape[0], : s_ref.shape[1]]
+    table_out = pltpu.make_async_copy(table_ref, s_ref, table_sem)
+    table_out.start()
+
+    def finish(n, carry):
+        copy_out(n).wait()
+        return carry
+
+    lax.fori_loop(0, rows // (PART * BLOCK), finish, 0)
+    table_out.wait()
 
 
 def scale_blocks(x):
     rows, columns = x.shape
+    bands, blocks = rows // BLOCK, columns // BLOCK
     return pl.pallas_call(
         scale_kernel,
         out_shape=(
             jax.ShapeDtypeStruct((rows, columns), x.dtype),
-            jax.ShapeDtypeStruct((columns // BLOCK, rows // BLOCK), jnp.float32),
+            jax.ShapeDtypeStruct((blocks, bands), jnp.float32),
         ),
         in_specs=[pl.BlockSpec(memory_space=pltpu.VMEM)],
         out_specs=(
             pl.BlockSpec(memory_space=pl.ANY),
-            pl.BlockSpec(memory_space=pltpu.VMEM),
+            pl.BlockSpec(memory_space=pl.ANY),
         ),
         scratch_shapes=[
             pltpu.VMEM((rows, columns), x.dtype),
-            pltpu.VMEM((BLOCK, BLOCK), jnp.float32),
-            pltpu.SemaphoreType.DMA((rows // (BANDS * BLOCK),)),
+            pltpu.VMEM((bands // BANDS, BANDS, BLOCK), jnp.float32),
+            pltpu.VMEM((blocks, bands), jnp.float32),
+            pltpu.SemaphoreType.DMA((bands // PART,)),
+            pltpu.SemaphoreType.DMA,
         ],
         compiler_params=pltpu.CompilerParams(vmem_limit_bytes=32 * 2**20),
         name="scale_blocks",

time: 104 us -> 103 us (level)
  no operation moved by 1% of the time
where the time goes in v5:
time: 103 us
  blocking collectives  97 us (94%)
  Pallas kernels  5.56 us (5%)
    all_to_all x1, blocking collectives, on_device(): lax.all_to_all(outgoing, ('fsdp', 'rep'), split_axis=0, concat_axis=0, ti...  97 us
    pallas_call x1, Pallas kernels, scale_blocks(): pl.pallas_call(scale_kernel, out_shape=(jax.ShapeDtypeStruct((rows, colum...  3.43 us
    pallas_call x1, Pallas kernels, arrange(): pl.pallas_call(arrange_kernel, out_shape=jax.ShapeDtypeStruct((experts *...  2.13 us

profile of v5, /device:TPU:1, one launch (start us, length us, event | category | flops | bytes accessed | tf_op | source)
XLA Modules:
  0.0 103.2 jit_solution(11493818841267511369)
XLA Ops:
  0.6 2.1 %arrange.1 = bf16[128,56,512]{2,1,0:T(8,128)(2,1)S(1)} custom-call(s32[8]{0:T(128)} %owner_hbm.1, bf16[8,56,4096]{2,1,0:T(8,128)(2,1)} %x_ref.1), custom_call_target="tpu_custom_call" | custom-call | tf_op jit(solution)/shard_map/arrange/pallas_call | solution.py:46
  2.8 97.0 %all_to_all.5 = bf16[128,56,512]{2,1,0:T(8,128)(2,1)S(1)} all-to-all(bf16[128,56,512]{2,1,0:T(8,128)(2,1)S(1)} %arrange.1), channel_id=1, replica_groups=mesh['fsdp'=64,'rep'=2] {'fsdp','rep'}, dimensions={0} | all-to-all | bytes 14680064 | tf_op jit(solution)/shard_map/all_to_all | solution.py:149
  99.7 3.4 %scale_blocks.1 = (bf16[7168,512]{1,0:T(8,128)(2,1)}, f32[4,56]{1,0:T(4,128)}) custom-call(bf16[7168,512]{1,0:T(8,128)(2,1)S(1)} %bitcast.5), custom_call_target="tpu_custom_call" | custom-call | tf_op jit(solution)/shard_map/scale_blocks/pallas_call | solution.py:122
